TPU v7x, 32 devices: a whole 2x2x4 slice. The times are simulated.
32 devices in a mesh: groups: 2 (over y), ctx: 4 (over z), head: 4 (over x, core).
Axes of the slice: x: 2, y: 2, z: 4, core: 2. Of those that a mesh axis runs over, the one named last changes fastest.
Arguments:
- q_nope: bfloat16 [1024, 12288], P(('groups', 'ctx'), 'head'), parts along dimension 0, may hold values from -6 to 6
- q_rope: bfloat16 [1024, 6144], P(('groups', 'ctx'), 'head'), parts along dimension 0, may hold values from -56 to 56
- w_uk: bfloat16 [96, 128, 512], P('head'), may hold values from -0.5 to 0.5
- w_uv: bfloat16 [96, 512, 128], P('head'), may hold values from -0.25 to 0.25
- cache_latent: bfloat16 [256, 64, 512], P(('groups', 'ctx')), parts along dimension 0, may hold values from -6 to 6
- cache_rope: bfloat16 [256, 4096], P(('groups', 'ctx')), parts along dimension 0, may hold values from -6 to 6
- block_owner: int32 [256], P('groups'), parts along dimension 0, may hold values from 0 to 3, as said below
- selection: int32 [64, 32], P(('groups', 'ctx')), parts along dimension 0, may hold values from 0 to 127, as said below
Outputs:
- attn_out: bfloat16 [1024, 12288], P(('groups', 'ctx'), 'head'), parts along dimension 0
There are 2 independent parts, one for each index of `groups`. A program takes and returns all parts, laid end to end along the dimension named above; an argument that names none is the same for every part. Nothing has to cross between parts.
Inputs may be any that keep to these rules, and one draw needn't show every extreme that they name: `selection`: row g serves queries g * 16 to g * 16 + 15 and names 32 different blocks: first the block that holds those queries, then the block before it, then blocks below (29) * 4. Over the 8 rows of one ctx index, at most 17 different blocks lie on any one owner, and on one owner, the same for every ctx index, exactly 17. `block_owner`: blocks k * 4 to k * 4 + 3 lie on 4 different owners; block b is row b // 4 of its owner's 32 rows.
All inputs are finite; a program needn't handle non-finite values.
Results may differ from a plain program's by a relative error of at most 0.0085.
Values may be sent and summed in bfloat16 or wider, within the bound.
A program may use at most 128 MiB of HBM per device.

v0:
```python
import jax
import jax.numpy as jnp
from jax import lax
from jax.sharding import PartitionSpec as P


def slot_lists(present, owned, capacity, owners):
    member = present * owned
    ranking = jnp.cumsum(member) - 1
    local_row = lax.broadcasted_iota(jnp.int32, present.shape, 0) // owners
    slot_ids = lax.broadcasted_iota(jnp.int32, (capacity,) + present.shape, 0)
    matched = (ranking[None, :] == slot_ids) & (member[None, :] > 0)
    listing = jnp.sum(jnp.where(matched, local_row[None, :], 0), axis=1)
    return (listing, jnp.where(member > 0, ranking, 0))


def on_device(q_nope, q_rope, w_uk, w_uv, cache_latent, cache_rope, block_owner, selection):
    owners = lax.axis_size("ctx")
    my_index = lax.axis_index("ctx")
    query_count = q_nope.shape[0]
    head_count = w_uk.shape[0]
    head_dim = w_uk.shape[1]
    latent = w_uk.shape[2]
    block_len = cache_latent.shape[1]
    rope_dim = cache_rope.shape[1] // block_len
    group_count = selection.shape[0]
    pick_count = selection.shape[1]
    block_count = block_owner.shape[0]
    query_blocks = query_count // block_len
    capacity = max(3 + query_blocks // 8, (2 * pick_count + 2 * query_blocks) // owners)
    group_size = query_count // group_count
    owner_ids = lax.broadcasted_iota(jnp.int32, (owners, block_count), 0)
    owned_all = (block_owner[None, :] == owner_ids).astype(jnp.int32)
    present = jnp.zeros((block_count,), jnp.int32).at[selection.reshape(-1)].set(1)
    listings, ranking = jax.vmap(lambda owned: slot_lists(present, owned, capacity, owners))(
        owned_all
    )
    position = block_owner * capacity + jnp.sum(ranking, axis=0)
    wanted = lax.all_to_all(listings, "ctx", split_axis=0, concat_axis=0, tiled=True)
    flat_rows = wanted.reshape(-1)
    lat_rows = cache_latent[flat_rows]
    rope_rows = cache_rope[flat_rows]
    lat_out = lat_rows.reshape(owners, capacity, block_len, latent)
    rope_out = rope_rows.reshape(owners, capacity, block_len * rope_dim)
    lat_in, rope_in = (
        lax.all_to_all(lat_out, "ctx", split_axis=0, concat_axis=0, tiled=True),
        lax.all_to_all(rope_out, "ctx", split_axis=0, concat_axis=0, tiled=True),
    )
    lat_keys = lat_in.reshape(owners * capacity, block_len, latent)
    rope_keys = rope_in.reshape(owners * capacity, block_len, rope_dim)
    where_sel = position[selection]
    keys_lat = lat_keys[where_sel].reshape(group_count, pick_count * block_len, latent)
    keys_rope = rope_keys[where_sel].reshape(group_count, pick_count * block_len, rope_dim)
    nope_rows = q_nope.reshape(query_count, head_count, head_dim)
    q_lat = jnp.einsum("qhd,hdc->qhc", nope_rows, w_uk, preferred_element_type=jnp.float32).astype(
        jnp.bfloat16
    )
    q_lat = q_lat.reshape(group_count, group_size, head_count, latent)
    rope_query = q_rope.reshape(group_count, group_size, head_count, rope_dim)
    softmax_scale = (head_dim + rope_dim) ** (-0.5)
    scores = jnp.einsum("gqhc,gkc->gqhk", q_lat, keys_lat, preferred_element_type=jnp.float32)
    scores = scores + jnp.einsum(
        "gqhr,gkr->gqhk", rope_query, keys_rope, preferred_element_type=jnp.float32
    )
    scores = scores * softmax_scale
    first_pos = block_count * block_len - query_count * owners + my_index * query_count
    query_pos = first_pos + jnp.arange(query_count, dtype=jnp.int32).reshape(
        group_count, group_size
    )
    token_ids = jnp.arange(block_len, dtype=jnp.int32)
    key_pos = (selection[:, :, None] * block_len + token_ids[None, None, :]).reshape(
        group_count, pick_count * block_len
    )
    allowed = key_pos[:, None, None, :] <= query_pos[:, :, None, None]
    scores = jnp.where(allowed, scores, -jnp.inf)
    row_max = jnp.max(scores, axis=-1, keepdims=True)
    shifted = jnp.exp(scores - row_max)
    weights = (shifted / jnp.sum(shifted, axis=-1, keepdims=True)).astype(jnp.bfloat16)
    out_latent = jnp.einsum(
        "gqhk,gkc->gqhc", weights, keys_lat, preferred_element_type=jnp.float32
    ).astype(jnp.bfloat16)
    out_latent = out_latent.reshape(query_count, head_count, latent)
    result = jnp.einsum(
        "qhc,hcv->qhv", out_latent, w_uv, preferred_element_type=jnp.float32
    ).astype(jnp.bfloat16)
    return result.reshape(query_count, head_count * w_uv.shape[2])


def solution(mesh):
    return jax.shard_map(
        on_device,
        mesh=mesh,
        in_specs=(
            P(("groups", "ctx"), "head"),
            P(("groups", "ctx"), "head"),
            P("head", None, None),
            P("head", None, None),
            P(("groups", "ctx"), None, None),
            P(("groups", "ctx"), None),
            P("groups"),
            P(("groups", "ctx"), None),
        ),
        out_specs=P(("groups", "ctx"), "head"),
        check_vma=False,
    )
```

profile of v0, /device:TPU:0, one launch (start us, length us, event | category | flops | bytes accessed | tf_op | source)
XLA Modules:
  0.0 248.2 jit_solution(7684383342076304130)
XLA Ops:
  0.0 0.9 reshape.186
  0.9 1.4 scatter_custom_fusion
  3.3 0.7 select_reduce_fusion.1
  4.5 11.7 %all_to_all.19 = s32[4,1,17]{2,1,0:T(1,128)S(1)} all-to-all(s32[4,1,17]{2,1,0:T(1,128)S(1)} %copy.31), channel_id=1, replica_groups=mesh['groups'=2,'ctx'=4,'head'=4] {'ctx'}, dimensions={0} | all-to-all | bytes 544 | tf_op jit(solution)/shard_map/all_to_all | solution.py:39
  16.6 0.7 reduce.3
  17.4 3.2 %gather_fusion.3 = bf16[68,4096]{1,0:T(8,128)(2,1)} fusion(bf16[32,4096]{1,0:T(8,128)(2,1)} %param.13, s32[1024]{0:T(1024)S(1)} %pad_clamp_fusion.2), kind=kCustom, calls=%fused_computation.3 | custom fusion | bytes 1114384 | tf_op jit(solution)/shard_map/gather | solution.py:42
  20.6 2.1 reshape.191
  22.7 4.2 %all-to-all-start.2 = ((bf16[4,17,4096]{2,1,0:T(8,128)(2,1)}), bf16[4,17,4096]{2,1,0:T(8,128)(2,1)}, u32[]{:S(2)}, u32[]{:S(2)}) async-start(bf16[4,17,4096]{2,1,0:T(8,128)(2,1)} %reshape.191), calls=%async_computation.2 | async-start | bytes 1572864 | tf_op jit(solution)/shard_map/all_to_all | solution.py:47
  26.9 7.0 %gather_fusion = bf16[68,64,512]{2,1,0:T(8,128)(2,1)} fusion(bf16[32,64,512]{2,1,0:T(8,128)(2,1)} %param.12, s32[1024]{0:T(1024)S(1)} %pad_clamp_fusion.2), kind=kCustom, calls=%fused_computation | custom fusion | bytes 8913168 | tf_op jit(solution)/shard_map/gather | solution.py:41
  34.0 12.0 %all-to-all-done.2 = bf16[4,17,4096]{2,1,0:T(8,128)(2,1)} async-done(((bf16[4,17,4096]{2,1,0:T(8,128)(2,1)}), bf16[4,17,4096]{2,1,0:T(8,128)(2,1)}, u32[]{:S(2)}, u32[]{:S(2)}) %all-to-all-start.2) | async-done | bytes 557088 | tf_op jit(solution)/shard_map/all_to_all | solution.py:47
  45.9 5.1 %all-to-all-start.1 = ((bf16[4,17,64,512]{3,2,1,0:T(8,128)(2,1)}), bf16[4,17,64,512]{3,2,1,0:T(8,128)(2,1)}, u32[]{:S(2)}, u32[]{:S(2)}) async-start(bf16[4,17,64,512]{3,2,1,0:T(8,128)(2,1)} %bitcast.49), calls=%async_computation.1 | async-start | bytes 8912896 | tf_op jit(solution)/shard_map/all_to_all | solution.py:46
  51.1 1.9 gather_fusion.1
  53.5 2.3 reshape.194
  55.8 3.8 %convolution_convert_fusion = bf16[24,512,128]{1,2,0:T(8,128)(2,1)} fusion(bf16[24,128,512]{2,1,0:T(8,128)(2,1)S(1)} %copy-done, bf16[128,3072]{1,0:T(8,128)(2,1)} %param.8), kind=kOutput, calls=%fused_computation.17 | convolution fusion | flops 404226048 | bytes 7077888 | tf_op jit(solution)/shard_map/qhd,hdc->qhc/dot_general | solution.py:55
  59.8 2.2 reshape.192
  62.1 3.0 %gather_fusion.4 = bf16[256,64,64]{2,1,0:T(8,128)(2,1)} fusion(bf16[68,64,64]{2,1,0:T(8,128)(2,1)S(1)} %reshape.192, s32[1024]{0:T(1024)S(1)} %pad_clamp_fusion), kind=kCustom, calls=%fused_computation.4 | custom fusion | bytes 4195328 | tf_op jit(solution)/shard_map/gather | solution.py:53
  65.1 84.1 %all-to-all-done.1 = bf16[4,17,64,512]{3,2,1,0:T(8,128)(2,1)} async-done(((bf16[4,17,64,512]{3,2,1,0:T(8,128)(2,1)}), bf16[4,17,64,512]{3,2,1,0:T(8,128)(2,1)}, u32[]{:S(2)}, u32[]{:S(2)}) %all-to-all-start.1) | async-done | bytes 4456480 | tf_op jit(solution)/shard_map/all_to_all | solution.py:46
  149.1 12.1 %gather_fusion.2 = bf16[256,64,512]{2,1,0:T(8,128)(2,1)} fusion(bf16[68,64,512]{2,1,0:T(8,128)(2,1)} %bitcast.6, s32[1024]{0:T(1024)S(1)} %pad_clamp_fusion), kind=kCustom, calls=%fused_computation.2 | custom fusion | bytes 33555456 | tf_op jit(solution)/shard_map/gather | solution.py:52
  161.3 15.2 %fusion.6 = f32[8,16,24,2048]{3,2,1,0:T(8,128)} fusion(bf16[8,2048,512,1]{2,1,3,0:T(8,128)(2,1)} %bitcast.46, bf16[8,16,24,512]{3,1,0,2:T(8,128)(2,1)S(1)} %bitcast.50), kind=kOutput, calls=%fused_computation.15 | convolution fusion | flops 6442450944 | bytes 45088768 | tf_op jit(solution)/shard_map/gqhc,gkc->gqhk/dot_general | solution.py:61
  176.5 18.9 %fusion.2 = f32[8,16,24,2048]{3,2,1,0:T(8,128)} fusion(f32[8,16,24,2048]{3,2,1,0:T(8,128)} %fusion.6, pred[8,16,2048]{2,1,0:T(8,128)(4,1)S(1)} %broadcast_compare_fusion, bf16[8,2048,64,1]{2,1,3,0:T(8,128)(2,1)} %bitcast.48, bf16[8,16,24,64]{3,2,1,0:T(8,128)(2,1)} %reshape.194), kind=kOutput, calls=%fused_computation.9 | convolution fusion | flops 824180736 | bytes 53084160 | tf_op jit(solution)/shard_map/gqhr,gkr->gqhk/dot_general | solution.py:62
  195.4 19.7 %fusion.20 = f32[8,16,24]{2,1,0:T(8,128)S(1)} fusion(f32[8,16,24,2048]{3,2,1,0:T(8,128)} %fusion.2), kind=kOutput, calls=%fused_computation.50 | output fusion | flops 12584959 | bytes 25178112 | tf_op jit(solution)/shard_map/sub | solution.py:77
  215.0 24.7 %fusion.8 = bf16[8,16,24,512]{3,2,1,0:T(8,128)(2,1)} fusion(bf16[8,2048,512,1]{2,1,3,0:T(8,128)(2,1)} %bitcast.47, f32[8,16,24]{2,1,0:T(8,128)S(1)} %fusion.20, f32[8,16,24,2048]{3,2,1,0:T(8,128)} %fusion.2), kind=kOutput, calls=%fused_computation.18 | convolution fusion | flops 6462903296 | bytes 45101056 | tf_op jit(solution)/shard_map/gqhk,gkc->gqhc/dot_general | solution.py:79
  239.7 6.1 %fusion.9 = bf16[24,128,128]{1,2,0:T(8,128)(2,1)} fusion(bf16[24,512,128]{2,1,0:T(8,128)(2,1)} %param.11, bf16[128,24,512]{2,1,0:T(8,128)(2,1)} %bitcast.54), kind=kOutput, calls=%fused_computation.19 | convolution fusion | flops 403046400 | bytes 7077888 | tf_op jit(solution)/shard_map/qhc,hcv->qhv/dot_general | solution.py:83
  245.9 2.3 copy.37
  (36 shorter events, 2.8 us)
Async XLA Ops:
  0.0 55.8 %copy-start = (bf16[24,128,512]{2,1,0:T(8,128)(2,1)S(1)}, bf16[24,128,512]{2,1,0:T(8,128)(2,1)}, u32[]{:S(2)}) copy-start(bf16[24,128,512]{2,1,0:T(8,128)(2,1)} %param.10) | copy-start | bytes 9437188
  22.7 23.2 %all-to-all-start.2 = ((bf16[4,17,4096]{2,1,0:T(8,128)(2,1)}), bf16[4,17,4096]{2,1,0:T(8,128)(2,1)}, u32[]{:S(2)}, u32[]{:S(2)}) async-start(bf16[4,17,4096]{2,1,0:T(8,128)(2,1)} %reshape.191), calls=%async_computation.2 | async-start | bytes 1572864 | tf_op jit(solution)/shard_map/all_to_all | solution.py:47
  34.0 17.1 %copy-start.3 = (s32[8,32]{1,0:T(8,128)S(1)}, s32[8,32]{1,0:T(8,128)}, u32[]{:S(2)}) copy-start(s32[8,32]{1,0:T(8,128)} %param.15) | copy-start | bytes 3076
  34.0 17.2 %copy-start.4 = (s32[128]{0:T(128)S(1)}, s32[128]{0:T(128)}, u32[]{:S(2)}) copy-start(s32[128]{0:T(128)} %param.14) | copy-start | bytes 1540
  45.9 103.2 %all-to-all-start.1 = ((bf16[4,17,64,512]{3,2,1,0:T(8,128)(2,1)}), bf16[4,17,64,512]{3,2,1,0:T(8,128)(2,1)}, u32[]{:S(2)}, u32[]{:S(2)}) async-start(bf16[4,17,64,512]{3,2,1,0:T(8,128)(2,1)} %bitcast.49), calls=%async_computation.1 | async-start | bytes 8912896 | tf_op jit(solution)/shard_map/all_to_all | solution.py:46
  149.1 12.1 %copy-start.2 = (bf16[24,512,128]{1,2,0:T(8,128)(2,1)S(1)}, bf16[24,512,128]{1,2,0:T(8,128)(2,1)}, u32[]{:S(2)}) copy-start(bf16[24,512,128]{1,2,0:T(8,128)(2,1)} %convolution_convert_fusion) | copy-start | bytes 9437188
  215.0 33.1 %copy-start.1 = (bf16[24,128,512]{2,1,0:T(8,128)(2,1)S(1)}, bf16[24,128,512]{2,1,0:T(8,128)(2,1)}, u32[]{:S(2)}) copy-start(bf16[24,128,512]{2,1,0:T(8,128)(2,1)} %param.10) | copy-start | bytes 9437188
where the time goes:
time: 249 us; the launch traced here: 248 us
  waiting for transfers between devices  96.1 us (39%)
  matrix products  68.7 us (28%)
  local copies, waits for them, and re-layouts  39.7 us (16%)
  other arithmetic  22.6 us (9%)
  blocking collectives  11.7 us (5%)
  starting transfers between devices  9.26 us (4%)
    all_to_all x1, waiting for transfers between devices, on_device(): lax.all_to_all(lat_out, 'ctx', split_axis=0, concat_axis=0, tiled=True)  84.1 us
    dot_general x1, matrix products, on_device(): jnp.einsum('gqhk,gkc->gqhc', weights, keys_lat, preferred_element_type=jn...  24.7 us
    sub x1, other arithmetic, on_device(): shifted = jnp.exp(scores - row_max)  19.7 us
    dot_general x1, matrix products, on_device(): jnp.einsum('gqhr,gkr->gqhk', rope_query, keys_rope, preferred_element_typ...  18.9 us
    dot_general x1, matrix products, on_device(): jnp.einsum('gqhc,gkc->gqhk', q_lat, keys_lat, preferred_element_type=jnp....  15.2 us
    gather x1, local copies, waits for them, and re-layouts, on_device(): lat_keys[where_sel].reshape(group_count, pick_count * block_len, latent)  12.1 us
    all_to_all x1, waiting for transfers between devices, on_device(): lax.all_to_all(rope_out, 'ctx', split_axis=0, concat_axis=0, tiled=True)  12 us
    all_to_all x1, blocking collectives, on_device(): lax.all_to_all(listings, 'ctx', split_axis=0, concat_axis=0, tiled=True)  11.7 us
  transfers between devices with their start and end apart: 2, of which 2 were waited for; matrix products, arithmetic and copies ran while one was open for 8% of the time, Pallas kernels for 0%

commit v1 on v0

v1 whole, which is shorter than its diff:
```python
import functools
import math

import jax
import jax.numpy as jnp
from jax import lax
from jax.experimental import pallas as pl
from jax.experimental.pallas import tpu as pltpu
from jax.sharding import PartitionSpec as P

LANES = 128
PIECES = 4
VMEM_BYTES = 56 * 1024 * 1024
MESH = pl.DeviceIdType.MESH


def slot_lists(present, owned, capacity, owners):
    member = present * owned
    ranking = jnp.cumsum(member) - 1
    local_row = lax.broadcasted_iota(jnp.int32, present.shape, 0) // owners
    slot_ids = lax.broadcasted_iota(jnp.int32, (capacity,) + present.shape, 0)
    matched = (ranking[None, :] == slot_ids) & (member[None, :] > 0)
    listing = jnp.sum(jnp.where(matched, local_row[None, :], 0), axis=1)
    return (listing, jnp.where(member > 0, ranking, 0))


def pack_blocks(latent_rows, rope_rows):
    rows, block_len, latent = latent_rows.shape
    lat = latent_rows.reshape(rows, block_len, latent // LANES, LANES)
    lat = lat.transpose(0, 2, 1, 3).reshape(rows, -1, LANES)
    return jnp.concatenate([lat, rope_rows], axis=1)


def split_rope(cache_rope, block_len):
    rows = cache_rope.shape[0]
    halves = cache_rope.reshape(rows, 2, block_len // 2, -1)
    return halves.transpose(0, 2, 1, 3).reshape(rows, block_len // 2, -1)


def project_queries(nope_ref, rope_ref, uk_ref, qfull_ref):
    head_count, head_dim, latent = uk_ref.shape
    groups = qfull_ref.shape[0]
    size = qfull_ref.shape[1] // head_count
    half = LANES // 2

    def one_pair(pair, carry):
        slab = rope_ref[:, pl.ds(pl.multiple_of(pair * LANES, LANES), LANES)].astype(jnp.float32)
        turned = pltpu.roll(slab, half, 1)
        low = lax.broadcasted_iota(jnp.int32, slab.shape, 1) < half
        twice = (jnp.where(low, slab, turned), jnp.where(low, turned, slab))
        for odd in range(2):
            head = pair * 2 + odd
            query = nope_ref[:, pl.ds(pl.multiple_of(head * head_dim, LANES), head_dim)]
            lat = jnp.dot(query, uk_ref[head], preferred_element_type=jnp.float32)
            lat = lat.astype(jnp.bfloat16).reshape(groups, size, latent)
            rot = twice[odd].astype(jnp.bfloat16).reshape(groups, size, LANES)
            at = pl.ds(pl.multiple_of(head * size, size), size)
            qfull_ref[:, at, :latent] = lat
            qfull_ref[:, at, latent:] = rot
        return carry

    lax.fori_loop(0, head_count // 2, one_pair, 0)


def query_kernel(nope_ref, rope_ref, uk_ref, qfull_ref):
    project_queries(nope_ref, rope_ref, uk_ref, qfull_ref)


def gather_kernel(
    ctx_size, head_size, nope_ref, rope_ref, uk_ref, lat_ref, krope_ref, all_ref, qfull_ref,
    packed, local_sem, right_send, right_recv, left_send, left_recv, x_send, x_recv, z_core_send, z_core_recv,
    x_core_send, x_core_recv,
):
    ctx = lax.axis_index("ctx")
    head = lax.axis_index("head")
    across = (head + head_size // 2) % head_size
    sibling = head + 1 - 2 * (head % 2)
    rows = lat_ref.shape[0]
    quarter = rows // head_size
    piece = quarter // PIECES
    block_len = lat_ref.shape[1]
    lane_groups = lat_ref.shape[2] // LANES
    has_left = ctx > 0
    has_right = ctx < ctx_size - 1

    barrier = pltpu.get_barrier_semaphore()
    pl.semaphore_signal(barrier, inc=1, device_id={"head": across}, device_id_type=MESH)
    pl.semaphore_signal(barrier, inc=1, device_id={"head": sibling}, device_id_type=MESH)

    @pl.when(has_left)
    def _():
        pl.semaphore_signal(barrier, inc=1, device_id={"ctx": ctx - 1}, device_id_type=MESH)

    @pl.when(has_right)
    def _():
        pl.semaphore_signal(barrier, inc=1, device_id={"ctx": ctx + 1}, device_id_type=MESH)

    def pack_row(row, carry):
        for group in range(lane_groups):
            packed[row, group * block_len:(group + 1) * block_len, :] = lat_ref[
                row, :, group * LANES:(group + 1) * LANES
            ]
        packed[row, lane_groups * block_len:, :] = krope_ref[row]
        return carry

    lax.fori_loop(0, rows, pack_row, 0)
    pl.semaphore_wait(barrier, 2 + has_left.astype(jnp.int32) + has_right.astype(jnp.int32))

    own = pltpu.make_async_copy(packed, all_ref.at[pl.ds(ctx * rows, rows)], local_sem)
    own.start()

    def place(shard, part, k):
        return all_ref.at[pl.ds(shard * rows + part * quarter + k * piece, piece)]

    def hop(source, target, send, recv, device):
        return pltpu.make_async_remote_copy(
            src_ref=source, dst_ref=target, send_sem=send, recv_sem=recv, device_id=device, device_id_type=MESH
        )

    def send_right(source, shard, k, at):
        return hop(source, place(shard, head, k), right_send.at[at], right_recv.at[at], {"ctx": ctx + 1})

    def send_left(source, shard, k, at):
        return hop(source, place(shard, head, k), left_send.at[at], left_recv.at[at], {"ctx": ctx - 1})

    def start_own(k, carry):
        source = packed.at[pl.ds(head * quarter + k * piece, piece)]

        @pl.when(has_right)
        def _():
            send_right(source, ctx, k, k).start()

        @pl.when(has_left)
        def _():
            send_left(source, ctx, k, k).start()

        return carry

    lax.fori_loop(0, PIECES, start_own, 0)
    project_queries(nope_ref, rope_ref, uk_ref, qfull_ref)

    events = (ctx_size - 1) * PIECES

    def x_copy(side, at, shard, k, part):
        ref = place(shard, part, k)
        return hop(ref, ref, x_send.at[side, at], x_recv.at[side, at], {"head": across})

    def z_core_copy(side, at, shard, k, part):
        ref = place(shard, part, k)
        return hop(ref, ref, z_core_send.at[side, at], z_core_recv.at[side, at], {"head": sibling})

    def x_core_copy(side, at, shard, k, part):
        ref = place(shard, part, k)
        return hop(ref, ref, x_core_send.at[side, at], x_core_recv.at[side, at], {"head": sibling})

    def sides(at):
        step = at // PIECES
        return (
            (0, ctx - 1 - step, ctx - 1 - step >= 0),
            (1, ctx + 1 + step, ctx + 1 + step <= ctx_size - 1),
        )

    def from_z(at):
        k = at % PIECES
        for side, shard, there in sides(at):

            @pl.when(there)
            def _(side=side, shard=shard):
                if side == 0:
                    send_right(place(shard, head, k), shard, k, at).wait_recv()

                    @pl.when(has_right)
                    def _():
                        send_right(place(shard, head, k), shard, k, at + PIECES).start()
                else:
                    send_left(place(shard, head, k), shard, k, at).wait_recv()

                    @pl.when(has_left)
                    def _():
                        send_left(place(shard, head, k), shard, k, at + PIECES).start()

                x_copy(side, at, shard, k, head).start()
                z_core_copy(side, at, shard, k, head).start()

    def from_x(at):
        k = at % PIECES
        for side, shard, there in sides(at):

            @pl.when(there)
            def _(side=side, shard=shard):
                x_copy(side, at, shard, k, across).wait_recv()
                x_core_copy(side, at, shard, k, across).start()

    def event(at, carry):
        @pl.when(at < events)
        def _():
            from_z(at)

        @pl.when(at > 0)
        def _():
            from_x(at - 1)

        return carry

    lax.fori_loop(0, events + 1, event, 0)
    own.wait()

    def finish(at, carry):
        k = at % PIECES
        sibling_across = (sibling + head_size // 2) % head_size
        for side, shard, there in sides(at):

            @pl.when(there)
            def _(side=side, shard=shard):
                z_core_copy(side, at, shard, k, sibling).wait_recv()
                x_core_copy(side, at, shard, k, sibling_across).wait_recv()
                x_copy(side, at, shard, k, head).wait_send()
                z_core_copy(side, at, shard, k, head).wait_send()
                x_core_copy(side, at, shard, k, across).wait_send()
                if side == 0:

                    @pl.when(has_right)
                    def _():
                        send_right(place(shard, head, k), shard, k, at + PIECES).wait_send()
                else:

                    @pl.when(has_left)
                    def _():
                        send_left(place(shard, head, k), shard, k, at + PIECES).wait_send()

        return carry

    lax.fori_loop(0, events, finish, 0)

    def finish_own(k, carry):
        source = packed.at[pl.ds(head * quarter + k * piece, piece)]

        @pl.when(has_right)
        def _():
            send_right(source, ctx, k, k).wait_send()

        @pl.when(has_left)
        def _():
            send_left(source, ctx, k, k).wait_send()

        return carry

    lax.fori_loop(0, PIECES, finish_own, 0)


def attend(block_rows, limit, q_ref, keys_ref, scores_ref, scale, block_len, latent, chunk):
    lane_groups = latent // LANES
    size = q_ref.shape[0]
    half = block_len // 2
    low = lax.broadcasted_iota(jnp.int32, (half, LANES), 1) < LANES // 2

    def values_of(row):
        return [
            keys_ref[row, group * block_len:(group + 1) * block_len, :] for group in range(lane_groups)
        ]

    def keys_of(row):
        rope = keys_ref[row, lane_groups * block_len:, :]
        zero = jnp.zeros_like(rope)
        both = jnp.concatenate([jnp.where(low, rope, zero), jnp.where(low, zero, rope)], axis=0)
        return values_of(row) + [both]

    def stack(rows, parts_of):
        return jnp.concatenate([jnp.concatenate(parts_of(row), axis=1) for row in rows], axis=0)

    width = chunk * block_len
    count = len(block_rows) // chunk
    query = q_ref[...]
    top = None
    for c in range(count):
        keys = stack(block_rows[c * chunk:(c + 1) * chunk], keys_of)
        score = lax.dot_general(query, keys, (((1,), (1,)), ((), ())), preferred_element_type=jnp.float32)
        if c == 0:
            head_part = score[:, :LANES]
            lane = lax.broadcasted_iota(jnp.int32, head_part.shape, 1)
            barred = (lane < block_len) & (lane > limit)
            score = jnp.concatenate([jnp.where(barred, -jnp.inf, head_part), score[:, LANES:]], axis=1)
        scores_ref[:, c * width:(c + 1) * width] = score
        for at in range(width // LANES):
            part = score[:, at * LANES:(at + 1) * LANES]
            top = part if top is None else jnp.maximum(top, part)
    factor = scale * math.log2(math.e)
    shift = jnp.max(top, axis=1, keepdims=True) * factor
    total = jnp.zeros((size, LANES), jnp.float32)
    out = jnp.zeros((size, latent), jnp.float32)
    for c in range(count):
        weight = jnp.exp2(scores_ref[:, c * width:(c + 1) * width] * factor - shift)
        for at in range(width // LANES):
            total = total + weight[:, at * LANES:(at + 1) * LANES]
        values = stack(block_rows[c * chunk:(c + 1) * chunk], values_of)
        out = out + jnp.dot(weight.astype(jnp.bfloat16), values, preferred_element_type=jnp.float32)
    return out / jnp.sum(total, axis=1, keepdims=True)


def attention_kernel(
    scale, block_len, rows_ref, limit_ref, qfull_ref, keys_ref, uv_ref, out_ref, scores, out_latent
):
    head_count, latent, value_dim = uv_ref.shape
    groups = qfull_ref.shape[0]
    size = qfull_ref.shape[1] // head_count
    picks = rows_ref.shape[1]

    def one_list(g, carry):
        block_rows = [rows_ref[g, j] for j in range(picks)]
        query_at = lax.broadcasted_iota(jnp.int32, (qfull_ref.shape[1], LANES), 0) % size
        limit = limit_ref[g] + query_at
        found = attend(
            block_rows, limit, qfull_ref.at[g], keys_ref, scores, scale, block_len, latent, 4
        )
        out_latent[g] = found.astype(jnp.bfloat16)
        return carry

    lax.fori_loop(0, groups, one_list, 0)

    def one_head(h, carry):
        part = out_latent[:, pl.ds(pl.multiple_of(h * size, size), size), :].reshape(groups * size, latent)
        result = jnp.dot(part, uv_ref[h], preferred_element_type=jnp.float32)
        out_ref[:, pl.ds(pl.multiple_of(h * value_dim, LANES), value_dim)] = result.astype(jnp.bfloat16)
        return carry

    lax.fori_loop(0, head_count, one_head, 0)


def on_device(q_nope, q_rope, w_uk, w_uv, cache_latent, cache_rope, block_owner, selection):
    owners = lax.axis_size("ctx")
    heads = lax.axis_size("head")
    my_index = lax.axis_index("ctx")
    query_count = q_nope.shape[0]
    head_count, head_dim, latent = w_uk.shape
    value_dim = w_uv.shape[2]
    cache_rows, block_len = cache_latent.shape[:2]
    rope_dim = cache_rope.shape[1] // block_len
    group_count, pick_count = selection.shape
    block_count = block_owner.shape[0]
    query_blocks = query_count // block_len
    capacity = max(3 + query_blocks // 8, (2 * pick_count + 2 * query_blocks) // owners)
    group_size = query_count // group_count
    block_ids = lax.broadcasted_iota(jnp.int32, (block_count,), 0)
    rope_rows = split_rope(cache_rope, block_len)
    packed_rows = latent // LANES * block_len + block_len // 2
    qfull_shape = jax.ShapeDtypeStruct((group_count, head_count * group_size, latent + LANES), jnp.bfloat16)
    vmem = pl.BlockSpec(memory_space=pltpu.VMEM)
    smem = pl.BlockSpec(memory_space=pltpu.SMEM)

    if cache_rows <= 2 * capacity:
        position = block_owner * cache_rows + block_ids // owners
        events = (owners - 1) * PIECES
        pairs = [pltpu.SemaphoreType.DMA((events + PIECES,))] * 4 + [pltpu.SemaphoreType.DMA((2, events))] * 6
        keys, qfull = pl.pallas_call(
            functools.partial(gather_kernel, owners, heads),
            out_shape=(
                jax.ShapeDtypeStruct((owners * cache_rows, packed_rows, LANES), jnp.bfloat16),
                qfull_shape,
            ),
            in_specs=[vmem] * 5,
            out_specs=(pl.BlockSpec(memory_space=pl.ANY), vmem),
            scratch_shapes=[
                pltpu.VMEM((cache_rows, packed_rows, LANES), jnp.bfloat16),
                pltpu.SemaphoreType.DMA(()),
            ] + pairs,
            compiler_params=pltpu.CompilerParams(
                collective_id=0, has_side_effects=True, vmem_limit_bytes=VMEM_BYTES
            ),
        )(q_nope, q_rope, w_uk, cache_latent, rope_rows)
    else:
        owner_ids = lax.broadcasted_iota(jnp.int32, (owners, block_count), 0)
        owned_all = (block_owner[None, :] == owner_ids).astype(jnp.int32)
        present = jnp.zeros((block_count,), jnp.int32).at[selection.reshape(-1)].set(1)
        listings, ranking = jax.vmap(lambda owned: slot_lists(present, owned, capacity, owners))(
            owned_all
        )
        position = block_owner * capacity + jnp.sum(ranking, axis=0)
        wanted = lax.all_to_all(listings, "ctx", split_axis=0, concat_axis=0, tiled=True)
        flat_rows = wanted.reshape(-1)
        asked = pack_blocks(cache_latent[flat_rows], rope_rows[flat_rows])
        asked = asked.reshape(owners, capacity, packed_rows, LANES)
        keys = lax.all_to_all(asked, "ctx", split_axis=0, concat_axis=0, tiled=True)
        keys = keys.reshape(owners * capacity, packed_rows, LANES)
        qfull = pl.pallas_call(
            query_kernel,
            out_shape=qfull_shape,
            in_specs=[vmem] * 3,
            out_specs=vmem,
            compiler_params=pltpu.CompilerParams(vmem_limit_bytes=VMEM_BYTES),
        )(q_nope, q_rope, w_uk)

    first_pos = block_count * block_len - query_count * owners + my_index * query_count
    limits = first_pos + jnp.arange(group_count, dtype=jnp.int32) * group_size - selection[:, 0] * block_len
    return pl.pallas_call(
        functools.partial(attention_kernel, (head_dim + rope_dim) ** (-0.5), block_len),
        out_shape=jax.ShapeDtypeStruct((query_count, head_count * value_dim), jnp.bfloat16),
        in_specs=[smem, smem, vmem, vmem, vmem],
        out_specs=vmem,
        scratch_shapes=[
            pltpu.VMEM((head_count * group_size, pick_count * block_len), jnp.float32),
            pltpu.VMEM((group_count, head_count * group_size, latent), jnp.bfloat16),
        ],
        compiler_params=pltpu.CompilerParams(vmem_limit_bytes=VMEM_BYTES),
    )(position[selection], limits, qfull, keys, w_uv)


def solution(mesh):
    return jax.shard_map(
        on_device,
        mesh=mesh,
        in_specs=(
            P(("groups", "ctx"), "head"),
            P(("groups", "ctx"), "head"),
            P("head", None, None),
            P("head", None, None),
            P(("groups", "ctx"), None, None),
            P(("groups", "ctx"), None),
            P("groups"),
            P(("groups", "ctx"), None),
        ),
        out_specs=P(("groups", "ctx"), "head"),
        check_vma=False,
    )
```

time: 249 us -> 102 us (0.41)
  waiting for transfers between devices: 96.1 us -> 0 us
  Pallas kernels: 0 us -> 94.3 us
  matrix products: 68.7 us -> 0 us
  local copies, waits for them, and re-layouts: 39.7 us -> 4.61 us
  other arithmetic: 22.6 us -> 2.71 us
  blocking collectives: 11.7 us -> 0 us
  starting transfers between devices: 9.26 us -> 0 us
    all_to_all x2 -> x0, waiting for transfers between devices: 96.1 us -> none  [the longest x1 84.1 us: on_device(): lax.all_to_all(lat_out, 'ctx', split_axis=0, concat_axis=0, tiled=True)]
    pallas_call x0 -> x2, Pallas kernels: none -> 94.3 us  [the longest x1 61.3 us: on_device(): pl.pallas_call(functools.partial(gather_kernel, owners, heads), out_shape...]
    dot_general x5 -> x0, matrix products: 68.7 us -> none  [the longest x1 24.7 us: on_device(): jnp.einsum('gqhk,gkc->gqhc', weights, keys_lat, preferred_element_type=jn...]
    gather x6 -> x2, local copies, waits for them, and re-layouts: 27.3 us -> 2.53 us  [on_device(): position[selection]]
    sub x1, other arithmetic: 19.7 us -> 0.51 us  [on_device(): first_pos + jnp.arange(group_count, dtype=jnp.int32) * group_size]
    all_to_all x1 -> x0, blocking collectives: 11.7 us -> none  [on_device(): lax.all_to_all(listings, 'ctx', split_axis=0, concat_axis=0, tiled=True)]
    all_to_all x2 -> x0, starting transfers between devices: 9.26 us -> none  [the longest x1 5.07 us: on_device(): lax.all_to_all(lat_out, 'ctx', split_axis=0, concat_axis=0, tiled=True)]
    reshape x6 -> x3, local copies, waits for them, and re-layouts: 9.97 us -> 2 us  [the longest x2 1.05 us: split_rope(): halves = cache_rope.reshape(rows, 2, block_len // 2, -1)]
  transfers between devices with their start and end apart: 2 -> 0, of which waited for: 2 -> 0; matrix products, arithmetic and copies ran while one was open for 8% -> 0% of each run, Pallas kernels for 0% -> 0%
where the time goes in v1:
time: 102 us
  Pallas kernels  94.3 us (92%)
  local copies, waits for them, and re-layouts  4.61 us (5%)
  other arithmetic  2.71 us (3%)
    pallas_call x1, Pallas kernels, on_device(): pl.pallas_call(functools.partial(gather_kernel, owners, heads), out_shape...  61.3 us
    pallas_call x1, Pallas kernels, on_device(): pl.pallas_call(functools.partial(attention_kernel, (head_dim + rope_dim)...  33 us
    gather x2, local copies, waits for them, and re-layouts, on_device(): position[selection]  2.53 us

profile of v1, /device:TPU:0, one launch (start us, length us, event | category | flops | bytes accessed | tf_op | source)
XLA Modules:
  0.0 101.7 jit_solution(4129370480754478389)
XLA Ops:
  0.0 0.0 copy-start
  0.0 0.7 fusion
  0.7 0.8 multiply_reduce_fusion
  1.5 0.5 add_subtract_fusion.limit_ref
  2.0 0.7 compare_select_fusion
  2.7 0.1 reshape.12
  2.8 1.9 %gather_fusion = s32[256]{0:T(256)S(1)} fusion(s32[128]{0:T(128)S(1)} %fusion, s32[1024]{0:T(1024)S(1)} %pad_clamp_fusion), kind=kCustom, calls=%fused_computation | custom fusion | bytes 3072 | tf_op jit(solution)/shard_map/gather | solution.py:404
  4.7 0.7 reshape.11.rows_ref
  5.3 0.0 copy-done
  5.3 0.5 reshape.8
  5.9 0.5 copy.12
  6.4 1.0 reshape.9.krope_ref
  7.4 61.3 %shard_map.82 = (bf16[128,288,128]{2,1,0:T(8,128)(2,1)}, bf16[8,384,640]{2,1,0:T(8,128)(2,1)}) custom-call(bf16[128,3072]{1,0:T(8,128)(2,1)} %nope_ref.1, bf16[128,1536]{1,0:T(8,128)(2,1)} %rope_ref.1, bf16[24,128,512]{2,1,0:T(8,128)(2,1)} %uk_ref.1, bf16[32,64,512]{2,1,0:T(8,128)(2,1)} %lat_ref.1, bf16[32,32,128]{2,1,0:T(8,128)(2,1)} %reshape.9.krope_ref), custom_call_target="tpu_custom_call" | custom-call | tf_op jit(solution)/shard_map/pallas_call | solution.py:354
  68.7 33.0 %shard_map.83 = bf16[128,3072]{1,0:T(8,128)(2,1)} custom-call(s32[8,32]{1,0:T(8,128)} %reshape.11.rows_ref, s32[8]{0:T(128)} %add_subtract_fusion.limit_ref, bf16[8,384,640]{2,1,0:T(8,128)(2,1)} %get-tuple-element.7.qfull_ref, bf16[128,288,128]{2,1,0:T(8,128)(2,1)} %get-tuple-element.8.keys_ref, bf16[24,512,128]{2,1,0:T(8,128)(2,1)} %uv_ref.1), custom_call_target="tpu_custom_call" | custom-call | tf_op jit(solution)/shard_map/pallas_call | solution.py:394
  (1 shorter events, 0.0 us)
Async XLA Ops:
  0.0 5.3 %copy-start = (bf16[32,4096]{1,0:T(8,128)(2,1)S(1)}, bf16[32,4096]{1,0:T(8,128)(2,1)}, u32[]{:S(2)}) copy-start(bf16[32,4096]{1,0:T(8,128)(2,1)} %param.13) | copy-start | bytes 786436

commit v2 on v1

v2 whole, which is shorter than its diff:
```python
import functools
import math

import jax
import jax.numpy as jnp
from jax import lax
from jax.experimental import pallas as pl
from jax.experimental.pallas import tpu as pltpu
from jax.sharding import PartitionSpec as P

LANES = 128
PIECES = 4
VMEM_BYTES = 56 * 1024 * 1024
MESH = pl.DeviceIdType.MESH


def slot_lists(present, owned, capacity, owners):
    member = present * owned
    ranking = jnp.cumsum(member) - 1
    local_row = lax.broadcasted_iota(jnp.int32, present.shape, 0) // owners
    slot_ids = lax.broadcasted_iota(jnp.int32, (capacity,) + present.shape, 0)
    matched = (ranking[None, :] == slot_ids) & (member[None, :] > 0)
    listing = jnp.sum(jnp.where(matched, local_row[None, :], 0), axis=1)
    return (listing, jnp.where(member > 0, ranking, 0))


def pack_blocks(latent_rows, rope_rows):
    rows, block_len, latent = latent_rows.shape
    lat = latent_rows.reshape(rows, block_len, latent // LANES, LANES)
    lat = lat.transpose(0, 2, 1, 3).reshape(rows, -1, LANES)
    return jnp.concatenate([lat, rope_rows], axis=1)


def split_rope(cache_rope, block_len):
    rows = cache_rope.shape[0]
    halves = cache_rope.reshape(rows, 2, block_len // 2, -1)
    return halves.transpose(0, 2, 1, 3).reshape(rows, block_len // 2, -1)


def project_queries(nope_ref, rope_ref, uk_ref, qfull_ref, first, end):
    head_count, head_dim, latent = uk_ref.shape
    groups = qfull_ref.shape[0]
    size = qfull_ref.shape[1] // head_count
    half = LANES // 2

    def one_pair(pair, carry):
        slab = rope_ref[:, pl.ds(pl.multiple_of(pair * LANES, LANES), LANES)].astype(jnp.float32)
        turned = pltpu.roll(slab, half, 1)
        low = lax.broadcasted_iota(jnp.int32, slab.shape, 1) < half
        twice = (jnp.where(low, slab, turned), jnp.where(low, turned, slab))
        for odd in range(2):
            head = pair * 2 + odd
            query = nope_ref[:, pl.ds(pl.multiple_of(head * head_dim, LANES), head_dim)]
            lat = jnp.dot(query, uk_ref[head], preferred_element_type=jnp.float32)
            lat = lat.astype(jnp.bfloat16).reshape(groups, size, latent)
            rot = twice[odd].astype(jnp.bfloat16).reshape(groups, size, LANES)
            at = pl.ds(pl.multiple_of(head * size, size), size)
            qfull_ref[:, at, :latent] = lat
            qfull_ref[:, at, latent:] = rot
        return carry

    lax.fori_loop(first, end, one_pair, 0)


def query_kernel(nope_ref, rope_ref, uk_ref, qfull_ref):
    project_queries(nope_ref, rope_ref, uk_ref, qfull_ref, 0, uk_ref.shape[0] // 2)


def order_lists(sel_ref, owner_ref, order_ref, owners, cache_rows, late_owner, first_pos, size, block_len):
    groups, picks = sel_ref.shape
    sel = sel_ref[...]
    lane = lax.broadcasted_iota(jnp.int32, (groups, picks), 1)

    def find(b, found):
        return jnp.where(sel == b, owner_ref[b], found)

    owner = lax.fori_loop(0, owner_ref.shape[0], find, jnp.zeros_like(sel))
    row = owner * cache_rows + sel // owners
    key = jnp.where(lane == 0, 2 * picks, jnp.where(owner == late_owner, picks, 0)) + lane
    rank = jnp.zeros_like(sel)
    for j in range(picks):
        rank = rank + (key[:, j:j + 1] < key).astype(jnp.int32)
    wide = lax.broadcasted_iota(jnp.int32, (groups, LANES), 1)
    placed = jnp.zeros((groups, LANES), jnp.int32)
    for j in range(picks):
        placed = placed + jnp.where(rank[:, j:j + 1] == wide, row[:, j:j + 1], 0)
    at = lax.broadcasted_iota(jnp.int32, (groups, LANES), 0)
    behind = first_pos + at * size - sel[:, 0:1] * block_len
    order_ref[...] = jnp.where(wide == LANES - 1, behind, placed)


def fused_kernel(
    ctx_size, head_size, capacity, scale, owner_ref, sel_ref, lat_ref, krope_ref, nope_hbm, rope_hbm, uk_hbm, uv_hbm,
    out_ref, all_ref, late_ref, nope_ref, rope_ref, uk_ref, uv_ref, qfull_ref, scores, partial, peaks, totals,
    order_vec, order, local_sem, right_send, right_recv, left_send, left_recv, x_send, x_recv, z_core_send, z_core_recv,
    x_core_send, x_core_recv,
):
    ctx = lax.axis_index("ctx")
    head = lax.axis_index("head")
    across = (head + head_size // 2) % head_size
    sibling = head + 1 - 2 * (head % 2)
    sibling_across = (sibling + head_size // 2) % head_size
    rows, block_len, latent = lat_ref.shape
    quarter = rows // head_size
    piece = quarter // PIECES
    lane_groups = latent // LANES
    head_count, _, value_dim = uv_ref.shape
    groups, picks = sel_ref.shape
    size = qfull_ref.shape[1] // head_count
    has_left = ctx > 0
    has_right = ctx < ctx_size - 1
    last = ctx_size - 2

    barrier = pltpu.get_barrier_semaphore()
    pl.semaphore_signal(barrier, inc=1, device_id={"head": across}, device_id_type=MESH)
    pl.semaphore_signal(barrier, inc=1, device_id={"head": sibling}, device_id_type=MESH)

    @pl.when(has_left)
    def _():
        pl.semaphore_signal(barrier, inc=1, device_id={"ctx": ctx - 1}, device_id_type=MESH)

    @pl.when(has_right)
    def _():
        pl.semaphore_signal(barrier, inc=1, device_id={"ctx": ctx + 1}, device_id_type=MESH)

    loads = [
        pltpu.make_async_copy(source, target, local_sem.at[at])
        for at, (source, target) in enumerate(
            ((nope_hbm, nope_ref), (rope_hbm, rope_ref), (uk_hbm, uk_ref), (uv_hbm, uv_ref))
        )
    ]
    for load in loads:
        load.start()

    def pack_row(row, carry):
        for group in range(lane_groups):
            all_ref[ctx * rows + row, group * block_len:(group + 1) * block_len, :] = lat_ref[
                row, :, group * LANES:(group + 1) * LANES
            ]
        all_ref[ctx * rows + row, lane_groups * block_len:, :] = krope_ref[row]
        return carry

    lax.fori_loop(0, rows, pack_row, 0)
    pl.semaphore_wait(barrier, 2 + has_left.astype(jnp.int32) + has_right.astype(jnp.int32))

    def place(shard, part, k, step):
        at = part * quarter + k * piece
        if step == last:
            return late_ref.at[pl.ds(at, piece)]
        return all_ref.at[pl.ds(shard * rows + at, piece)]

    def hop(source, target, send, recv, device):
        return pltpu.make_async_remote_copy(
            src_ref=source, dst_ref=target, send_sem=send, recv_sem=recv, device_id=device, device_id_type=MESH
        )

    def z_copy(side, shard, k, step):
        source = place(shard, head, k, step - 1)
        target = place(shard, head, k, step)
        at = step * PIECES + k
        if side == 0:
            return hop(source, target, right_send.at[at], right_recv.at[at], {"ctx": ctx + 1})
        return hop(source, target, left_send.at[at], left_recv.at[at], {"ctx": ctx - 1})

    def local_copy(side, shard, k, step, part, send, recv, device):
        ref = place(shard, part, k, step)
        at = step * PIECES + k
        return hop(ref, ref, send.at[side, at], recv.at[side, at], {"head": device})

    def x_copy(side, shard, k, step, part):
        return local_copy(side, shard, k, step, part, x_send, x_recv, across)

    def z_core_copy(side, shard, k, step, part):
        return local_copy(side, shard, k, step, part, z_core_send, z_core_recv, sibling)

    def x_core_copy(side, shard, k, step, part):
        return local_copy(side, shard, k, step, part, x_core_send, x_core_recv, sibling)

    def sides(step):
        return (
            (0, ctx - 1 - step, ctx - 1 - step >= 0, has_right),
            (1, ctx + 1 + step, ctx + 1 + step <= ctx_size - 1, has_left),
        )

    def start_own(k, carry):
        @pl.when(has_right)
        def _():
            z_copy(0, ctx, k, 0).start()

        @pl.when(has_left)
        def _():
            z_copy(1, ctx, k, 0).start()

        return carry

    def from_z(step, k):
        for side, shard, there, onward in sides(step):

            @pl.when(there)
            def _(side=side, shard=shard, onward=onward):
                z_copy(side, shard, k, step).wait_recv()
                if step < last:

                    @pl.when(onward)
                    def _():
                        z_copy(side, shard, k, step + 1).start()

                x_copy(side, shard, k, step, head).start()
                z_core_copy(side, shard, k, step, head).start()

    def from_x(step, k):
        for side, shard, there, onward in sides(step):

            @pl.when(there)
            def _(side=side, shard=shard):
                x_copy(side, shard, k, step, across).wait_recv()
                x_core_copy(side, shard, k, step, across).start()

    def from_core(step, k):
        for side, shard, there, onward in sides(step):

            @pl.when(there)
            def _(side=side, shard=shard):
                z_core_copy(side, shard, k, step, sibling).wait_recv()
                x_core_copy(side, shard, k, step, sibling_across).wait_recv()

    lax.fori_loop(0, PIECES, start_own, 0)
    position = owner_ref.shape[0] * block_len - groups * size * ctx_size + ctx * groups * size
    late_owner = jnp.where(has_left & has_right, -1, ctx_size - 1 - ctx)
    order_lists(sel_ref, owner_ref, order_vec, ctx_size, rows, late_owner, position, size, block_len)
    to_scalar = pltpu.make_async_copy(order_vec, order, local_sem.at[4])
    to_scalar.start()
    for load in loads[:3]:
        load.wait()
    pairs = head_count // 2
    early_events = max(1, last * PIECES)
    share = -(-pairs // early_events)

    def project(at):
        project_queries(
            nope_ref, rope_ref, uk_ref, qfull_ref,
            jnp.minimum(at * share, pairs), jnp.minimum((at + 1) * share, pairs),
        )

    if last == 0:
        project(0)

    def run_step(step, with_project):
        def event(k, carry):
            from_z(step, k)
            if with_project:
                project(step * PIECES + k)

            @pl.when(k > 0)
            def _():
                from_x(step, k - 1)

            return carry

        lax.fori_loop(0, PIECES, event, 0)

    for step in range(last):
        if step > 0:
            from_x(step - 1, PIECES - 1)
        run_step(step, True)
    if last > 0:
        from_x(last - 1, PIECES - 1)

    def settle(step):
        lax.fori_loop(0, PIECES, lambda k, carry: (from_core(step, k), carry)[1], 0)

    for step in range(last):
        settle(step)
    to_scalar.wait()

    chunk = 4
    early = (picks - min(capacity, rows) - 1) // chunk * chunk if last > 0 else 0
    factor = scale * math.log2(math.e)

    def lists(first, count, final, service):
        def one_list(g, carry):
            block_rows = [order[g, first + j] for j in range(count)]
            query_at = lax.broadcasted_iota(jnp.int32, (qfull_ref.shape[1], LANES), 0) % size
            limit = order[g, LANES - 1] + query_at if final else None
            before = None if first == 0 else (peaks, totals, partial)
            peak, total, value = attend_part(
                g, before, block_rows, limit, qfull_ref, all_ref, scores, factor, block_len, latent, chunk
            )
            if final:
                found = value / jnp.sum(total, axis=1, keepdims=True)
                qfull_ref[g, :, :latent] = found.astype(jnp.bfloat16)
            else:
                peaks[g] = jnp.broadcast_to(peak, peaks.shape[1:])
                totals[g] = total
                partial[g] = value
            if service:
                every = max(1, groups // 2)

                @pl.when((g + 1) % every == 0)
                def _():
                    k = (g + 1) // every - 1

                    @pl.when(k < PIECES)
                    def _():
                        from_z(last, k)

                        @pl.when(k > 0)
                        def _():
                            from_x(last, k - 1)

            return carry

        lax.fori_loop(0, groups, one_list, 0)

    served = 0
    if early > 0:
        lists(0, early, False, True)
        served = min(PIECES, groups // max(1, groups // 2))

    def tail_event(k, carry):
        from_z(last, k)

        @pl.when(k > 0)
        def _():
            from_x(last, k - 1)

        return carry

    lax.fori_loop(served, PIECES, tail_event, 0)
    from_x(last, PIECES - 1)
    settle(last)

    @pl.when(late_owner >= 0)
    def _():
        def move(row, carry):
            all_ref[late_owner * rows + row] = late_ref[row]
            return carry

        lax.fori_loop(0, rows, move, 0)

    lists(early, picks - early, True, False)
    loads[3].wait()

    def one_head(h, carry):
        part = qfull_ref[:, pl.ds(pl.multiple_of(h * size, size), size), :latent].reshape(groups * size, latent)
        result = jnp.dot(part, uv_ref[h], preferred_element_type=jnp.float32)
        out_ref[:, pl.ds(pl.multiple_of(h * value_dim, LANES), value_dim)] = result.astype(jnp.bfloat16)
        return carry

    lax.fori_loop(0, head_count, one_head, 0)

    def finish(k, carry):
        @pl.when(has_right)
        def _():
            z_copy(0, ctx, k, 0).wait_send()

        @pl.when(has_left)
        def _():
            z_copy(1, ctx, k, 0).wait_send()

        for step in range(ctx_size - 1):
            for side, shard, there, onward in sides(step):

                @pl.when(there)
                def _(side=side, shard=shard, onward=onward, step=step):
                    x_copy(side, shard, k, step, head).wait_send()
                    z_core_copy(side, shard, k, step, head).wait_send()
                    x_core_copy(side, shard, k, step, across).wait_send()
                    if step < last:

                        @pl.when(onward)
                        def _():
                            z_copy(side, shard, k, step + 1).wait_send()

        return carry

    lax.fori_loop(0, PIECES, finish, 0)


def attend_part(g, before, block_rows, limit, qfull_ref, keys_ref, scores_ref, factor, block_len, latent, chunk):
    lane_groups = latent // LANES
    size = qfull_ref.shape[1]
    half = block_len // 2
    low = lax.broadcasted_iota(jnp.int32, (half, LANES), 1) < LANES // 2

    def values_of(row):
        return [
            keys_ref[row, group * block_len:(group + 1) * block_len, :] for group in range(lane_groups)
        ]

    def keys_of(row):
        rope = keys_ref[row, lane_groups * block_len:, :]
        zero = jnp.zeros_like(rope)
        both = jnp.concatenate([jnp.where(low, rope, zero), jnp.where(low, zero, rope)], axis=0)
        return values_of(row) + [both]

    def stack(rows, parts_of):
        return jnp.concatenate([jnp.concatenate(parts_of(row), axis=1) for row in rows], axis=0)

    width = chunk * block_len
    count = len(block_rows) // chunk
    query = qfull_ref[g]
    top = None
    for c in range(count):
        keys = stack(block_rows[c * chunk:(c + 1) * chunk], keys_of)
        score = lax.dot_general(query, keys, (((1,), (1,)), ((), ())), preferred_element_type=jnp.float32)
        if limit is not None and c == count - 1:
            end_part = score[:, width - LANES:]
            token = lax.broadcasted_iota(jnp.int32, end_part.shape, 1) - (LANES - block_len)
            end_part = jnp.where(token > limit, -jnp.inf, end_part)
            end_part = jnp.where(token < 0, score[:, width - LANES:], end_part)
            score = jnp.concatenate([score[:, :width - LANES], end_part], axis=1)
        scores_ref[:, c * width:(c + 1) * width] = score
        for at in range(width // LANES):
            piece = score[:, at * LANES:(at + 1) * LANES]
            top = piece if top is None else jnp.maximum(top, piece)
    peak = jnp.max(top, axis=1, keepdims=True)
    if before is None:
        total = jnp.zeros((size, LANES), jnp.float32)
        out = None
    else:
        peaks, totals, partial = before
        old = peaks[g][:, :1]
        peak = jnp.maximum(peak, old)
        fade = jnp.exp2((old - peak) * factor)
        total = totals[g] * fade
        out = partial[g] * fade
    shift = peak * factor
    for c in range(count):
        weight = jnp.exp2(scores_ref[:, c * width:(c + 1) * width] * factor - shift)
        for at in range(width // LANES):
            total = total + weight[:, at * LANES:(at + 1) * LANES]
        values = stack(block_rows[c * chunk:(c + 1) * chunk], values_of)
        more = jnp.dot(weight.astype(jnp.bfloat16), values, preferred_element_type=jnp.float32)
        out = more if out is None else out + more
    return peak, total, out


def attend(block_rows, limit, q_ref, keys_ref, scores_ref, scale, block_len, latent, chunk):
    lane_groups = latent // LANES
    size = q_ref.shape[0]
    half = block_len // 2
    low = lax.broadcasted_iota(jnp.int32, (half, LANES), 1) < LANES // 2

    def values_of(row):
        return [
            keys_ref[row, group * block_len:(group + 1) * block_len, :] for group in range(lane_groups)
        ]

    def keys_of(row):
        rope = keys_ref[row, lane_groups * block_len:, :]
        zero = jnp.zeros_like(rope)
        both = jnp.concatenate([jnp.where(low, rope, zero), jnp.where(low, zero, rope)], axis=0)
        return values_of(row) + [both]

    def stack(rows, parts_of):
        return jnp.concatenate([jnp.concatenate(parts_of(row), axis=1) for row in rows], axis=0)

    width = chunk * block_len
    count = len(block_rows) // chunk
    query = q_ref[...]
    top = None
    for c in range(count):
        keys = stack(block_rows[c * chunk:(c + 1) * chunk], keys_of)
        score = lax.dot_general(query, keys, (((1,), (1,)), ((), ())), preferred_element_type=jnp.float32)
        if c == 0:
            head_part = score[:, :LANES]
            lane = lax.broadcasted_iota(jnp.int32, head_part.shape, 1)
            barred = (lane < block_len) & (lane > limit)
            score = jnp.concatenate([jnp.where(barred, -jnp.inf, head_part), score[:, LANES:]], axis=1)
        scores_ref[:, c * width:(c + 1) * width] = score
        for at in range(width // LANES):
            part = score[:, at * LANES:(at + 1) * LANES]
            top = part if top is None else jnp.maximum(top, part)
    factor = scale * math.log2(math.e)
    shift = jnp.max(top, axis=1, keepdims=True) * factor
    total = jnp.zeros((size, LANES), jnp.float32)
    out = jnp.zeros((size, latent), jnp.float32)
    for c in range(count):
        weight = jnp.exp2(scores_ref[:, c * width:(c + 1) * width] * factor - shift)
        for at in range(width // LANES):
            total = total + weight[:, at * LANES:(at + 1) * LANES]
        values = stack(block_rows[c * chunk:(c + 1) * chunk], values_of)
        out = out + jnp.dot(weight.astype(jnp.bfloat16), values, preferred_element_type=jnp.float32)
    return out / jnp.sum(total, axis=1, keepdims=True)


def attention_kernel(
    scale, block_len, rows_ref, limit_ref, qfull_ref, keys_ref, uv_ref, out_ref, scores, out_latent
):
    head_count, latent, value_dim = uv_ref.shape
    groups = qfull_ref.shape[0]
    size = qfull_ref.shape[1] // head_count
    picks = rows_ref.shape[1]

    def one_list(g, carry):
        block_rows = [rows_ref[g, j] for j in range(picks)]
        query_at = lax.broadcasted_iota(jnp.int32, (qfull_ref.shape[1], LANES), 0) % size
        limit = limit_ref[g] + query_at
        found = attend(
            block_rows, limit, qfull_ref.at[g], keys_ref, scores, scale, block_len, latent, 4
        )
        out_latent[g] = found.astype(jnp.bfloat16)
        return carry

    lax.fori_loop(0, groups, one_list, 0)

    def one_head(h, carry):
        part = out_latent[:, pl.ds(pl.multiple_of(h * size, size), size), :].reshape(groups * size, latent)
        result = jnp.dot(part, uv_ref[h], preferred_element_type=jnp.float32)
        out_ref[:, pl.ds(pl.multiple_of(h * value_dim, LANES), value_dim)] = result.astype(jnp.bfloat16)
        return carry

    lax.fori_loop(0, head_count, one_head, 0)


def on_device(q_nope, q_rope, w_uk, w_uv, cache_latent, cache_rope, block_owner, selection):
    owners = lax.axis_size("ctx")
    heads = lax.axis_size("head")
    my_index = lax.axis_index("ctx")
    query_count = q_nope.shape[0]
    head_count, head_dim, latent = w_uk.shape
    value_dim = w_uv.shape[2]
    cache_rows, block_len = cache_latent.shape[:2]
    rope_dim = cache_rope.shape[1] // block_len
    group_count, pick_count = selection.shape
    block_count = block_owner.shape[0]
    query_blocks = query_count // block_len
    capacity = max(3 + query_blocks // 8, (2 * pick_count + 2 * query_blocks) // owners)
    group_size = query_count // group_count
    block_ids = lax.broadcasted_iota(jnp.int32, (block_count,), 0)
    rope_rows = split_rope(cache_rope, block_len)
    packed_rows = latent // LANES * block_len + block_len // 2
    qfull_shape = jax.ShapeDtypeStruct((group_count, head_count * group_size, latent + LANES), jnp.bfloat16)
    vmem = pl.BlockSpec(memory_space=pltpu.VMEM)
    smem = pl.BlockSpec(memory_space=pltpu.SMEM)

    out_shape = jax.ShapeDtypeStruct((query_count, head_count * value_dim), jnp.bfloat16)
    scale = (head_dim + rope_dim) ** (-0.5)

    if cache_rows <= 2 * capacity:
        events = (owners - 1) * PIECES
        width = head_count * group_size
        anywhere = pl.BlockSpec(memory_space=pl.ANY)
        return pl.pallas_call(
            functools.partial(fused_kernel, owners, heads, capacity, scale),
            out_shape=out_shape,
            in_specs=[smem, vmem, vmem, vmem] + [anywhere] * 4,
            out_specs=vmem,
            scratch_shapes=[
                pltpu.VMEM((owners * cache_rows, packed_rows, LANES), jnp.bfloat16),
                pltpu.VMEM((cache_rows, packed_rows, LANES), jnp.bfloat16),
                pltpu.VMEM(q_nope.shape, jnp.bfloat16),
                pltpu.VMEM(q_rope.shape, jnp.bfloat16),
                pltpu.VMEM(w_uk.shape, jnp.bfloat16),
                pltpu.VMEM(w_uv.shape, jnp.bfloat16),
                pltpu.VMEM(qfull_shape.shape, jnp.bfloat16),
                pltpu.VMEM((width, pick_count * block_len), jnp.float32),
                pltpu.VMEM((group_count, width, latent), jnp.float32),
                pltpu.VMEM((group_count, width, LANES), jnp.float32),
                pltpu.VMEM((group_count, width, LANES), jnp.float32),
                pltpu.VMEM((group_count, LANES), jnp.int32),
                pltpu.SMEM((group_count, LANES), jnp.int32),
                pltpu.SemaphoreType.DMA((5,)),
            ] + [pltpu.SemaphoreType.DMA((events,))] * 4 + [pltpu.SemaphoreType.DMA((2, events))] * 6,
            compiler_params=pltpu.CompilerParams(
                collective_id=0, has_side_effects=True, vmem_limit_bytes=VMEM_BYTES
            ),
        )(block_owner, selection, cache_latent, rope_rows, q_nope, q_rope, w_uk, w_uv)
    owner_ids = lax.broadcasted_iota(jnp.int32, (owners, block_count), 0)
    owned_all = (block_owner[None, :] == owner_ids).astype(jnp.int32)
    present = jnp.zeros((block_count,), jnp.int32).at[selection.reshape(-1)].set(1)
    listings, ranking = jax.vmap(lambda owned: slot_lists(present, owned, capacity, owners))(
        owned_all
    )
    position = block_owner * capacity + jnp.sum(ranking, axis=0)
    wanted = lax.all_to_all(listings, "ctx", split_axis=0, concat_axis=0, tiled=True)
    flat_rows = wanted.reshape(-1)
    asked = pack_blocks(cache_latent[flat_rows], rope_rows[flat_rows])
    asked = asked.reshape(owners, capacity, packed_rows, LANES)
    keys = lax.all_to_all(asked, "ctx", split_axis=0, concat_axis=0, tiled=True)
    keys = keys.reshape(owners * capacity, packed_rows, LANES)
    qfull = pl.pallas_call(
        query_kernel,
        out_shape=qfull_shape,
        in_specs=[vmem] * 3,
        out_specs=vmem,
        compiler_params=pltpu.CompilerParams(vmem_limit_bytes=VMEM_BYTES),
    )(q_nope, q_rope, w_uk)

    first_pos = block_count * block_len - query_count * owners + my_index * query_count
    limits = first_pos + jnp.arange(group_count, dtype=jnp.int32) * group_size - selection[:, 0] * block_len
    return pl.pallas_call(
        functools.partial(attention_kernel, scale, block_len),
        out_shape=out_shape,
        in_specs=[smem, smem, vmem, vmem, vmem],
        out_specs=vmem,
        scratch_shapes=[
            pltpu.VMEM((head_count * group_size, pick_count * block_len), jnp.float32),
            pltpu.VMEM((group_count, head_count * group_size, latent), jnp.bfloat16),
        ],
        compiler_params=pltpu.CompilerParams(vmem_limit_bytes=VMEM_BYTES),
    )(position[selection], limits, qfull, keys, w_uv)


def solution(mesh):
    return jax.shard_map(
        on_device,
        mesh=mesh,
        in_specs=(
            P(("groups", "ctx"), "head"),
            P(("groups", "ctx"), "head"),
            P("head", None, None),
            P("head", None, None),
            P(("groups", "ctx"), None, None),
            P(("groups", "ctx"), None),
            P("groups"),
            P(("groups", "ctx"), None),
        ),
        out_specs=P(("groups", "ctx"), "head"),
        check_vma=False,
    )
```

time: 102 us -> 99.4 us (0.975)
  other arithmetic: 2.71 us -> 0 us
    gather x2 -> x0, local copies, waits for them, and re-layouts: 2.53 us -> none  [on_device(): position[selection]]
    unnamed x2 -> x1, local copies, waits for them, and re-layouts: 0.01 us -> 2.06 us
    pallas_call x2 -> x1, Pallas kernels: 94.3 us -> 94.2 us  [on_device(): pl.pallas_call(functools.partial(fused_kernel, owners, heads, capacity, s...]
where the time goes in v2:
time: 99.4 us; the launch traced here: 99.2 us
  Pallas kernels  94.2 us (95%)
  local copies, waits for them, and re-layouts  5.01 us (5%)
    pallas_call x1, Pallas kernels, on_device(): pl.pallas_call(functools.partial(fused_kernel, owners, heads, capacity, s...  94.2 us
    unnamed x1, local copies, waits for them, and re-layouts  2.06 us

profile of v2, /device:TPU:0, one launch (start us, length us, event | category | flops | bytes accessed | tf_op | source)
XLA Modules:
  0.0 99.2 jit_solution(3443699442317340243)
XLA Ops:
  0.0 1.5 %reshape.6 = bf16[32,2,32,64]{3,2,1,0:T(8,128)(2,1)S(1)} reshape(bf16[32,4096]{1,0:T(8,128)(2,1)} %param.13) | data formatting | bytes 524288 | tf_op jit(solution)/shard_map/reshape | solution.py:36
  1.5 0.5 copy.11
  2.0 1.0 reshape.7.krope_ref
  3.0 94.2 %shard_map.82 = bf16[128,3072]{1,0:T(8,128)(2,1)} custom-call(s32[128]{0:T(128)} %owner_ref.1, s32[8,32]{1,0:T(8,128)} %sel_ref.1, bf16[32,64,512]{2,1,0:T(8,128)(2,1)} %lat_ref.1, bf16[32,32,128]{2,1,0:T(8,128)(2,1)} %reshape.7.krope_ref, bf16[128,3072]{1,0:T(8,128)(2,1)} %nope_hbm.1, bf16[128,1536]{1,0:T(8,128)(2,1)} %rope_hbm.1, ...), custom_call_target="tpu_custom_call" | custom-call | tf_op jit(solution)/shard_map/pallas_call | solution.py:545
  97.2 2.1 %copy.13 = bf16[128,3072]{1,0:T(8,128)(2,1)} copy(bf16[128,3072]{1,0:T(8,128)(2,1)} %shard_map.82) | data formatting | bytes 1572864

commit v3 on v2

--- a/solution.py
+++ b/solution.py
@@ -91,7 +91,7 @@
 
 def fused_kernel(
     ctx_size, head_size, capacity, scale, owner_ref, sel_ref, lat_ref, krope_ref, nope_hbm, rope_hbm, uk_hbm, uv_hbm,
-    out_ref, all_ref, late_ref, nope_ref, rope_ref, uk_ref, uv_ref, qfull_ref, scores, partial, peaks, totals,
+    out_ref, all_ref, late_ref, nope_ref, rope_ref, uk_ref, uv_ref, qfull_ref, found_ref, scores, more_scores, partial, peaks, totals, fades,
     order_vec, order, local_sem, right_send, right_recv, left_send, left_recv, x_send, x_recv, z_core_send, z_core_recv,
     x_core_send, x_core_recv,
 ):
@@ -278,44 +278,94 @@
     factor = scale * math.log2(math.e)
 
     def lists(first, count, final, service):
-        def one_list(g, carry):
-            block_rows = [order[g, first + j] for j in range(count)]
-            query_at = lax.broadcasted_iota(jnp.int32, (qfull_ref.shape[1], LANES), 0) % size
-            limit = order[g, LANES - 1] + query_at if final else None
-            before = None if first == 0 else (peaks, totals, partial)
-            peak, total, value = attend_part(
-                g, before, block_rows, limit, qfull_ref, all_ref, scores, factor, block_len, latent, chunk
-            )
+        steps = count // chunk
+        query_at = lax.broadcasted_iota(jnp.int32, (qfull_ref.shape[1], LANES), 0) % size
+
+        def rows_of(g):
+            return [order[g, first + j] for j in range(count)]
+
+        def limit_of(g):
+            return order[g, LANES - 1] + query_at if final else None
+
+        def store_top(g, top):
+            peak = jnp.max(top, axis=1, keepdims=True)
+            if first > 0:
+                old = peaks[g]
+                peak = jnp.maximum(peak, old[:, :1])
+                fades[...] = jnp.exp2((old - peak) * factor)
+            peaks[g] = jnp.broadcast_to(peak, peaks.shape[1:])
+
+        def score(g, buffer):
+            block_rows = rows_of(g)
+            top = None
+            for c in range(steps):
+                top = score_step(
+                    g, block_rows, limit_of(g), c, qfull_ref, all_ref, buffer, block_len, latent, chunk, top
+                )
+            store_top(g, top)
+
+        def both(g, buffer, then, then_buffer):
+            block_rows = rows_of(g)
+            shift = peaks[g][:, :1] * factor
+            if first > 0:
+                fade = fades[:, :1]
+                total, value = totals[g] * fade, partial[g] * fade
+            else:
+                total, value = jnp.zeros(totals.shape[1:], jnp.float32), None
+            then_rows = None if then is None else rows_of(then)
+            top = None
+            for c in range(steps):
+                if then is not None:
+                    top = score_step(
+                        then, then_rows, limit_of(then), c, qfull_ref, all_ref, then_buffer, block_len, latent,
+                        chunk, top,
+                    )
+                total, value = weigh_step(
+                    block_rows, c, all_ref, buffer, factor, shift, block_len, latent, chunk, total, value
+                )
             if final:
                 found = value / jnp.sum(total, axis=1, keepdims=True)
-                qfull_ref[g, :, :latent] = found.astype(jnp.bfloat16)
+                found_ref[g] = found.astype(jnp.bfloat16)
             else:
-                peaks[g] = jnp.broadcast_to(peak, peaks.shape[1:])
                 totals[g] = total
                 partial[g] = value
+            if then is not None:
+                store_top(then, top)
+
+        def serve(k):
+            from_z(last, k)
+
+            @pl.when(k > 0)
+            def _():
+                from_x(last, k - 1)
+
+        score(0, scores)
+
+        def two_lists(pair, carry):
+            both(2 * pair, scores, 2 * pair + 1, more_scores)
+
+            @pl.when(pair < groups // 2 - 1)
+            def _():
+                both(2 * pair + 1, more_scores, 2 * pair + 2, scores)
+
+            @pl.when(pair == groups // 2 - 1)
+            def _():
+                both(2 * pair + 1, more_scores, None, None)
+
             if service:
-                every = max(1, groups // 2)
-
-                @pl.when((g + 1) % every == 0)
+
+                @pl.when((pair == 1) | (pair == 3))
                 def _():
-                    k = (g + 1) // every - 1
-
-                    @pl.when(k < PIECES)
-                    def _():
-                        from_z(last, k)
-
-                        @pl.when(k > 0)
-                        def _():
-                            from_x(last, k - 1)
+                    serve(pair // 2)
 
             return carry
 
-        lax.fori_loop(0, groups, one_list, 0)
+        lax.fori_loop(0, groups // 2, two_lists, 0)
 
     served = 0
     if early > 0:
         lists(0, early, False, True)
-        served = min(PIECES, groups // max(1, groups // 2))
+        served = groups // 4
 
     def tail_event(k, carry):
         from_z(last, k)
@@ -342,7 +392,7 @@
     loads[3].wait()
 
     def one_head(h, carry):
-        part = qfull_ref[:, pl.ds(pl.multiple_of(h * size, size), size), :latent].reshape(groups * size, latent)
+        part = found_ref[:, pl.ds(pl.multiple_of(h * size, size), size), :].reshape(groups * size, latent)
         result = jnp.dot(part, uv_ref[h], preferred_element_type=jnp.float32)
         out_ref[:, pl.ds(pl.multiple_of(h * value_dim, LANES), value_dim)] = result.astype(jnp.bfloat16)
         return carry
@@ -377,63 +427,49 @@
     lax.fori_loop(0, PIECES, finish, 0)
 
 
-def attend_part(g, before, block_rows, limit, qfull_ref, keys_ref, scores_ref, factor, block_len, latent, chunk):
+def score_step(g, block_rows, limit, c, qfull_ref, keys_ref, scores_ref, block_len, latent, chunk, top):
     lane_groups = latent // LANES
-    size = qfull_ref.shape[1]
     half = block_len // 2
     low = lax.broadcasted_iota(jnp.int32, (half, LANES), 1) < LANES // 2
-
-    def values_of(row):
-        return [
-            keys_ref[row, group * block_len:(group + 1) * block_len, :] for group in range(lane_groups)
-        ]
+    width = chunk * block_len
 
     def keys_of(row):
         rope = keys_ref[row, lane_groups * block_len:, :]
         zero = jnp.zeros_like(rope)
         both = jnp.concatenate([jnp.where(low, rope, zero), jnp.where(low, zero, rope)], axis=0)
-        return values_of(row) + [both]
-
-    def stack(rows, parts_of):
-        return jnp.concatenate([jnp.concatenate(parts_of(row), axis=1) for row in rows], axis=0)
-
+        parts = [keys_ref[row, group * block_len:(group + 1) * block_len, :] for group in range(lane_groups)]
+        return jnp.concatenate(parts + [both], axis=1)
+
+    keys = jnp.concatenate([keys_of(row) for row in block_rows[c * chunk:(c + 1) * chunk]], axis=0)
+    score = lax.dot_general(
+        qfull_ref[g], keys, (((1,), (1,)), ((), ())), preferred_element_type=jnp.float32
+    )
+    if limit is not None and (c + 1) * chunk == len(block_rows):
+        end_part = score[:, width - LANES:]
+        token = lax.broadcasted_iota(jnp.int32, end_part.shape, 1) - (LANES - block_len)
+        end_part = jnp.where((token >= 0) & (token > limit), -jnp.inf, end_part)
+        score = jnp.concatenate([score[:, :width - LANES], end_part], axis=1)
+    scores_ref[:, c * width:(c + 1) * width] = score
+    for at in range(width // LANES):
+        piece = score[:, at * LANES:(at + 1) * LANES]
+        top = piece if top is None else jnp.maximum(top, piece)
+    return top
+
+
+def weigh_step(block_rows, c, keys_ref, scores_ref, factor, shift, block_len, latent, chunk, total, out):
+    lane_groups = latent // LANES
     width = chunk * block_len
-    count = len(block_rows) // chunk
-    query = qfull_ref[g]
-    top = None
-    for c in range(count):
-        keys = stack(block_rows[c * chunk:(c + 1) * chunk], keys_of)
-        score = lax.dot_general(query, keys, (((1,), (1,)), ((), ())), preferred_element_type=jnp.float32)
-        if limit is not None and c == count - 1:
-            end_part = score[:, width - LANES:]
-            token = lax.broadcasted_iota(jnp.int32, end_part.shape, 1) - (LANES - block_len)
-            end_part = jnp.where(token > limit, -jnp.inf, end_part)
-            end_part = jnp.where(token < 0, score[:, width - LANES:], end_part)
-            score = jnp.concatenate([score[:, :width - LANES], end_part], axis=1)
-        scores_ref[:, c * width:(c + 1) * width] = score
-        for at in range(width // LANES):
-            piece = score[:, at * LANES:(at + 1) * LANES]
-            top = piece if top is None else jnp.maximum(top, piece)
-    peak = jnp.max(top, axis=1, keepdims=True)
-    if before is None:
-        total = jnp.zeros((size, LANES), jnp.float32)
-        out = None
-    else:
-        peaks, totals, partial = before
-        old = peaks[g][:, :1]
-        peak = jnp.maximum(peak, old)
-        fade = jnp.exp2((old - peak) * factor)
-        total = totals[g] * fade
-        out = partial[g] * fade
-    shift = peak * factor
-    for c in range(count):
-        weight = jnp.exp2(scores_ref[:, c * width:(c + 1) * width] * factor - shift)
-        for at in range(width // LANES):
-            total = total + weight[:, at * LANES:(at + 1) * LANES]
-        values = stack(block_rows[c * chunk:(c + 1) * chunk], values_of)
-        more = jnp.dot(weight.astype(jnp.bfloat16), values, preferred_element_type=jnp.float32)
-        out = more if out is None else out + more
-    return peak, total, out
+
+    def values_of(row):
+        parts = [keys_ref[row, group * block_len:(group + 1) * block_len, :] for group in range(lane_groups)]
+        return jnp.concatenate(parts, axis=1)
+
+    weight = jnp.exp2(scores_ref[:, c * width:(c + 1) * width] * factor - shift)
+    for at in range(width // LANES):
+        total = total + weight[:, at * LANES:(at + 1) * LANES]
+    values = jnp.concatenate([values_of(row) for row in block_rows[c * chunk:(c + 1) * chunk]], axis=0)
+    more = jnp.dot(weight.astype(jnp.bfloat16), values, preferred_element_type=jnp.float32)
+    return total, more if out is None else out + more
 
 
 def attend(block_rows, limit, q_ref, keys_ref, scores_ref, scale, block_len, latent, chunk):
@@ -555,10 +591,13 @@
                 pltpu.VMEM(w_uk.shape, jnp.bfloat16),
                 pltpu.VMEM(w_uv.shape, jnp.bfloat16),
                 pltpu.VMEM(qfull_shape.shape, jnp.bfloat16),
+                pltpu.VMEM((group_count, width, latent), jnp.bfloat16),
+                pltpu.VMEM((width, pick_count * block_len), jnp.float32),
                 pltpu.VMEM((width, pick_count * block_len), jnp.float32),
                 pltpu.VMEM((group_count, width, latent), jnp.float32),
                 pltpu.VMEM((group_count, width, LANES), jnp.float32),
                 pltpu.VMEM((group_count, width, LANES), jnp.float32),
+                pltpu.VMEM((width, LANES), jnp.float32),
                 pltpu.VMEM((group_count, LANES), jnp.int32),
                 pltpu.SMEM((group_count, LANES), jnp.int32),
                 pltpu.SemaphoreType.DMA((5,)),

time: 99.4 us -> 86.9 us (0.87)
  Pallas kernels: 94.2 us -> 81.7 us
    pallas_call x1, Pallas kernels: 94.2 us -> 81.7 us  [on_device(): pl.pallas_call(functools.partial(fused_kernel, owners, heads, capacity, s...]
where the time goes in v3:
time: 86.9 us; the launch traced here: 86.7 us
  Pallas kernels  81.7 us (94%)
  local copies, waits for them, and re-layouts  5.01 us (6%)
    pallas_call x1, Pallas kernels, on_device(): pl.pallas_call(functools.partial(fused_kernel, owners, heads, capacity, s...  81.7 us
    unnamed x1, local copies, waits for them, and re-layouts  2.06 us
    reshape x2, local copies, waits for them, and re-layouts, split_rope(): halves = cache_rope.reshape(rows, 2, block_len // 2, -1)  1.99 us

profile of v3, /device:TPU:0, one launch (start us, length us, event | category | flops | bytes accessed | tf_op | source)
XLA Modules:
  0.0 86.7 jit_solution(9344286037488591966)
XLA Ops:
  0.0 1.5 %reshape.6 = bf16[32,2,32,64]{3,2,1,0:T(8,128)(2,1)S(1)} reshape(bf16[32,4096]{1,0:T(8,128)(2,1)} %param.13) | data formatting | bytes 524288 | tf_op jit(solution)/shard_map/reshape | solution.py:36
  1.5 0.5 copy.11
  2.0 1.0 %reshape.7.krope_ref = bf16[32,32,128]{2,1,0:T(8,128)(2,1)} reshape(bf16[32,32,2,64]{3,2,1,0:T(2,128)(2,1)S(1)} %bitcast.3) | data formatting | bytes 524288 | tf_op jit(solution)/shard_map/reshape | solution.py:37
  3.0 81.7 %shard_map.82 = bf16[128,3072]{1,0:T(8,128)(2,1)} custom-call(s32[128]{0:T(128)} %owner_ref.1, s32[8,32]{1,0:T(8,128)} %sel_ref.1, bf16[32,64,512]{2,1,0:T(8,128)(2,1)} %lat_ref.1, bf16[32,32,128]{2,1,0:T(8,128)(2,1)} %reshape.7.krope_ref, bf16[128,3072]{1,0:T(8,128)(2,1)} %nope_hbm.1, bf16[128,1536]{1,0:T(8,128)(2,1)} %rope_hbm.1, ...), custom_call_target="tpu_custom_call" | custom-call | tf_op jit(solution)/shard_map/pallas_call | solution.py:581
  84.6 2.1 %copy.13 = bf16[128,3072]{1,0:T(8,128)(2,1)} copy(bf16[128,3072]{1,0:T(8,128)(2,1)} %shard_map.82) | data formatting | bytes 1572864

commit v4 on v3

--- a/solution.py
+++ b/solution.py
@@ -137,7 +137,10 @@
             all_ref[ctx * rows + row, group * block_len:(group + 1) * block_len, :] = lat_ref[
                 row, :, group * LANES:(group + 1) * LANES
             ]
-        all_ref[ctx * rows + row, lane_groups * block_len:, :] = krope_ref[row]
+        rope = krope_ref[row]
+        all_ref[ctx * rows + row, lane_groups * block_len:, :] = jnp.concatenate(
+            [rope[:block_len // 2], rope[block_len // 2:]], axis=1
+        )
         return carry
 
     lax.fori_loop(0, rows, pack_row, 0)
@@ -565,7 +568,6 @@
     capacity = max(3 + query_blocks // 8, (2 * pick_count + 2 * query_blocks) // owners)
     group_size = query_count // group_count
     block_ids = lax.broadcasted_iota(jnp.int32, (block_count,), 0)
-    rope_rows = split_rope(cache_rope, block_len)
     packed_rows = latent // LANES * block_len + block_len // 2
     qfull_shape = jax.ShapeDtypeStruct((group_count, head_count * group_size, latent + LANES), jnp.bfloat16)
     vmem = pl.BlockSpec(memory_space=pltpu.VMEM)
@@ -605,7 +607,8 @@
             compiler_params=pltpu.CompilerParams(
                 collective_id=0, has_side_effects=True, vmem_limit_bytes=VMEM_BYTES
             ),
-        )(block_owner, selection, cache_latent, rope_rows, q_nope, q_rope, w_uk, w_uv)
+        )(block_owner, selection, cache_latent, cache_rope.reshape(cache_rows, block_len, rope_dim), q_nope, q_rope, w_uk, w_uv)
+    rope_rows = split_rope(cache_rope, block_len)
     owner_ids = lax.broadcasted_iota(jnp.int32, (owners, block_count), 0)
     owned_all = (block_owner[None, :] == owner_ids).astype(jnp.int32)
     present = jnp.zeros((block_count,), jnp.int32).at[selection.reshape(-1)].set(1)

time: 86.9 us -> 87.1 us (level)
  Pallas kernels: 81.7 us -> 82.6 us
    pallas_call x1, Pallas kernels: 81.7 us -> 82.6 us  [on_device(): pl.pallas_call(functools.partial(fused_kernel, owners, heads, capacity, s...]
    reshape x3 -> x1, local copies, waits for them, and re-layouts: 2.94 us -> 2.27 us  [on_device(): cache_rope.reshape(cache_rows, block_len, rope_dim)]
where the time goes in v4:
time: 87.1 us; the launch traced here: 86.9 us
  Pallas kernels  82.6 us (95%)
  local copies, waits for them, and re-layouts  4.33 us (5%)
    pallas_call x1, Pallas kernels, on_device(): pl.pallas_call(functools.partial(fused_kernel, owners, heads, capacity, s...  82.6 us
    reshape x1, local copies, waits for them, and re-layouts, on_device(): cache_rope.reshape(cache_rows, block_len, rope_dim)  2.27 us
    unnamed x1, local copies, waits for them, and re-layouts  2.06 us

profile of v4, /device:TPU:0, one launch (start us, length us, event | category | flops | bytes accessed | tf_op | source)
XLA Modules:
  0.0 86.9 jit_solution(3316587147549495229)
XLA Ops:
  0.0 2.3 %reshape.3.krope_ref = bf16[32,64,64]{2,1,0:T(8,128)(2,1)} reshape(bf16[32,4096]{1,0:T(8,128)(2,1)} %param.13) | data formatting | bytes 524288 | tf_op jit(solution)/shard_map/reshape | solution.py:610
  2.3 82.6 %shard_map.82 = bf16[128,3072]{1,0:T(8,128)(2,1)} custom-call(s32[128]{0:T(128)} %owner_ref.1, s32[8,32]{1,0:T(8,128)} %sel_ref.1, bf16[32,64,512]{2,1,0:T(8,128)(2,1)} %lat_ref.1, bf16[32,64,64]{2,1,0:T(8,128)(2,1)} %reshape.3.krope_ref, bf16[128,3072]{1,0:T(8,128)(2,1)} %nope_hbm.1, bf16[128,1536]{1,0:T(8,128)(2,1)} %rope_hbm.1, ...), custom_call_target="tpu_custom_call" | custom-call | tf_op jit(solution)/shard_map/pallas_call | solution.py:583
  84.8 2.1 %copy.10 = bf16[128,3072]{1,0:T(8,128)(2,1)} copy(bf16[128,3072]{1,0:T(8,128)(2,1)} %shard_map.82) | data formatting | bytes 1572864
